TPU v7x, 32 devices: a whole 2x2x4 slice. The times are simulated.
32 devices in a mesh: tm: 8 (over z, y), cell: 4 (over x, core).
Axes of the slice: x: 2, y: 2, z: 4, core: 2. Of those that a mesh axis runs over, the one named last changes fastest.
Arguments:
- increments: int32 [768, 8192], P('cell', 'tm'), may hold values from 0 to 3
- noise: bfloat16 [768, 8192], P('cell', 'tm'), may hold values from -6 to 6
- noise_scale: float32 [768], P('cell'), may hold values from 0.5 to 4
- factor: bfloat16 [8192], replicated, may hold values from 0 to 2
Outputs:
- counts: int32 [768, 8192], P('cell', 'tm')
- correlated_noise: float32 [768, 8192], P('cell', 'tm')
- total_counts: int32 [8192], P('tm')
All inputs are finite; a program needn't handle non-finite values.
Results may differ from a plain program's by a relative error of at most 0.0009.
Values may be sent and summed in bfloat16 or wider, within the bound.
A program may use at most 64 MiB of HBM per device.

v0:
```python
import jax
import jax.numpy as jnp
from jax import lax
from jax.sharding import PartitionSpec as P

BLK = 512


def prefix(value, axis, combine, identity):
    length, mine = (lax.axis_size(axis), lax.axis_index(axis))
    everything = lax.all_gather(value, axis)
    start = jnp.broadcast_to(jnp.asarray(identity, value.dtype), value.shape)

    def lap(k, before):
        reached = k < mine
        new = combine(before, everything[k])
        return jnp.where(reached, new, before)

    return lax.fori_loop(0, length, lap, start)


def partner(block, axis, distance):
    count = lax.axis_size(axis)
    route = []
    for low in range(count):
        high = low | 1 << distance
        if high != low and high < count:
            route += [(low, high), (high, low)]
    return lax.ppermute(block, axis, route)


def toeplitz(padded, zero_pad, first_offset, rows_count, cols_count):
    period = rows_count + cols_count - 1
    forward_part = lax.dynamic_slice_in_dim(padded, zero_pad + first_offset, cols_count)
    behind = lax.dynamic_slice_in_dim(
        padded, zero_pad + first_offset - (rows_count - 1), rows_count - 1
    )
    pattern = jnp.concatenate([forward_part, behind])
    repeated = jnp.tile(pattern, rows_count)[: rows_count * (period - 1)]
    return repeated.reshape(rows_count, period - 1)[:, :cols_count]


def add_counts(earlier, later):
    return earlier + later


def shards(increments, noise, noise_scale, factor):
    local_sums = jnp.cumsum(increments, axis=1, dtype=jnp.int32)
    cells_here = increments.shape[0]
    carried = prefix(local_sums[:, -1], "tm", add_counts, jnp.zeros((cells_here,), jnp.int32))
    counts = local_sums + carried[:, None]
    group_sums = lax.all_gather(
        jnp.sum(counts, axis=0, dtype=jnp.int32)[None, :], "cell", axis=0, tiled=True
    )
    total_counts = jnp.sum(group_sums, axis=0, dtype=jnp.int32)
    zero_pad = factor.shape[0]
    padded = jnp.concatenate([jnp.zeros_like(factor), factor])
    position = lax.axis_index("tm")
    devices = lax.axis_size("tm")
    segment = noise.shape[1]
    block_len = BLK
    own_begin = position * segment
    half_count = devices // 2
    quarter_count = devices // 4
    lower_half = position < half_count
    partner_begin = (position + half_count) * segment
    empty_pair = (
        jnp.zeros((cells_here, segment), jnp.float32),
        jnp.zeros((cells_here, segment), jnp.float32),
    )
    pieces = lax.all_gather(noise, "tm", axis=1, tiled=True)

    def one_block(index_block, totals):
        own_acc, far_acc = totals
        source_begin = index_block * block_len
        source_block = lax.dynamic_slice_in_dim(pieces, index_block * block_len, block_len, 1)
        source_device = source_begin // segment

        def product(target_begin):
            matrix = toeplitz(padded, zero_pad, target_begin - source_begin, block_len, segment)
            return jnp.dot(source_block, matrix, preferred_element_type=jnp.float32)

        def add_own(accum):
            return accum + product(own_begin)

        def add_far(accum):
            return accum + product(partner_begin)

        def keep_same(accum):
            return accum

        need_own = source_begin < own_begin + segment
        need_own = jnp.logical_and(
            need_own, jnp.logical_or(lower_half, source_device >= quarter_count)
        )
        need_far = jnp.logical_and(lower_half, source_device < quarter_count)
        far_acc = lax.cond(need_far, add_far, keep_same, far_acc)
        own_acc = lax.cond(need_own, add_own, keep_same, own_acc)
        return (own_acc, far_acc)

    own_acc, far_acc = lax.fori_loop(0, pieces.shape[1] // block_len, one_block, empty_pair)
    top_bit = devices.bit_length() - 2
    returned = partner(far_acc.astype(jnp.bfloat16), "tm", top_bit).astype(far_acc.dtype)
    own_acc = own_acc + returned
    correlated_noise = noise_scale[:, None] * own_acc
    return (counts, correlated_noise, total_counts)


def solution(mesh):
    return jax.shard_map(
        shards,
        mesh=mesh,
        in_specs=(P("cell", "tm"), P("cell", "tm"), P("cell"), P()),
        out_specs=(P("cell", "tm"), P("cell", "tm"), P("tm")),
        check_vma=False,
    )
```

profile of v0, /device:TPU:28, one launch (start us, length us, event | category | flops | bytes accessed | tf_op | source)
XLA Modules:
  0.0 205.8 jit_solution(922037539304337026)
XLA Ops:
  7.9 1.3 copy.15
  9.7 47.6 %fusion.4 = s32[192,8,128]{0,1,2:T(8,128)S(1)} fusion(s32[192,8,128]{0,1,2:T(8,128)S(1)} %copy.12), kind=kOutput, calls=%fused_computation.18 | output fusion | flops 24969216 | bytes 1572864 | tf_op jit(solution)/shard_map/reduce-window
  60.2 9.0 %all-reduce.1 = s32[1536]{0:T(1024)S(1)} all-reduce(s32[1536]{0:T(1024)S(1)} %dynamic-update-slice), channel_id=2, replica_groups=mesh['tm'=8,'cell'=4] {'tm'}, use_global_device_ids=true, to_apply=%add.1 | all-reduce | flops 1536 | bytes 12288
  69.7 1.0 broadcast.20
  70.7 1.0 broadcast.20.clone
  71.7 112.9 %while.37 = (s32[]{:T(128)}, f32[192,1024]{1,0:T(8,128)}, f32[192,1024]{1,0:T(8,128)}, s32[]{:T(128)}, pred[]{:T(512)}, /*index=5*/bf16[192,8192]{1,0:T(8,128)(2...) while((s32[]{:T(128)}, f32[192,1024]{1,0:T(8,128)}, ...), condition=%wide.region_9.10_spmd, body=%wide.region_4.9_spmd.sunk | while | flops 403058720 | bytes 28058292 | solution.py:101
  72.7 0.9 constant_dynamic-slice_fusion.4
  73.8 0.9 constant_dynamic-slice_fusion.4
  74.8 0.9 constant_dynamic-slice_fusion.4
  75.9 0.9 constant_dynamic-slice_fusion.4
  76.9 8.1 %conditional.4 = (f32[192,1024]{1,0:T(8,128)}) conditional(s32[]{:T(128)} %convert_element_type.31, f32[192,1024]{1,0:T(8,128)} %get-tuple-element.500, (s32[]{:T(128)}, s32[]{:T(128)}, bf16[16384]{0:T(1024)(128)(2,1)S(1)}, bf16[192,512]{1,0:T(8,128)(2,1)S(1)}, f32[192,1024]{1,0:T(8,128)}) %tuple.94), branch_computations={%region_5.5_spmd, %region_6.6_spmd} | conditional | flops 201529344 | bytes 13832302 | solution.py:98
  77.2 2.6 %tile.10 = bf16[785920]{0:T(1024)(128)(2,1)S(1)} reshape(bf16[512,1535]{1,0:T(8,128)(2,1)S(1)} %tile.4) | data formatting | bytes 3143680 | tf_op jit(solution)/shard_map/while/body/eval_jaxpr/cond/branch_1_fun/tile | solution.py:39
  79.9 2.6 %reshape.28 = bf16[512,1534]{1,0:T(8,128)(2,1)S(1)} reshape(bf16[785408]{0:T(1024)(128)(2,1)S(1)} %slice.24) | data formatting | bytes 3141632 | tf_op jit(solution)/shard_map/while/body/eval_jaxpr/cond/branch_1_fun/reshape | solution.py:40
  82.6 2.4 %fusion = f32[192,1024]{1,0:T(8,128)} fusion(f32[192,1024]{1,0:T(8,128)} %get-tuple-element.314, bf16[192,512]{1,0:T(8,128)(2,1)S(1)} %get-tuple-element.318, bf16[512,1534]{1,0:T(8,128)(2,1)S(1)} %reshape.28), kind=kOutput, calls=%fused_computation.1 | convolution fusion | flops 201523200 | bytes 2818048 | tf_op jit(solution)/shard_map/while/body/eval_jaxpr/cond/branch_1_fun/dot_general | solution.py:81
  85.9 8.1 %conditional.4 = (f32[192,1024]{1,0:T(8,128)}) conditional(s32[]{:T(128)} %convert_element_type.31, f32[192,1024]{1,0:T(8,128)} %get-tuple-element.500, (s32[]{:T(128)}, s32[]{:T(128)}, bf16[16384]{0:T(1024)(128)(2,1)S(1)}, bf16[192,512]{1,0:T(8,128)(2,1)S(1)}, f32[192,1024]{1,0:T(8,128)}) %tuple.94), branch_computations={%region_5.5_spmd, %region_6.6_spmd} | conditional | flops 201529344 | bytes 13832302 | solution.py:98
  86.3 2.6 %tile.10 = bf16[785920]{0:T(1024)(128)(2,1)S(1)} reshape(bf16[512,1535]{1,0:T(8,128)(2,1)S(1)} %tile.4) | data formatting | bytes 3143680 | tf_op jit(solution)/shard_map/while/body/eval_jaxpr/cond/branch_1_fun/tile | solution.py:39
  89.0 2.6 %reshape.28 = bf16[512,1534]{1,0:T(8,128)(2,1)S(1)} reshape(bf16[785408]{0:T(1024)(128)(2,1)S(1)} %slice.24) | data formatting | bytes 3141632 | tf_op jit(solution)/shard_map/while/body/eval_jaxpr/cond/branch_1_fun/reshape | solution.py:40
  91.6 2.4 %fusion = f32[192,1024]{1,0:T(8,128)} fusion(f32[192,1024]{1,0:T(8,128)} %get-tuple-element.314, bf16[192,512]{1,0:T(8,128)(2,1)S(1)} %get-tuple-element.318, bf16[512,1534]{1,0:T(8,128)(2,1)S(1)} %reshape.28), kind=kOutput, calls=%fused_computation.1 | convolution fusion | flops 201523200 | bytes 2818048 | tf_op jit(solution)/shard_map/while/body/eval_jaxpr/cond/branch_1_fun/dot_general | solution.py:81
  95.0 8.1 %conditional.4 = (f32[192,1024]{1,0:T(8,128)}) conditional(s32[]{:T(128)} %convert_element_type.31, f32[192,1024]{1,0:T(8,128)} %get-tuple-element.500, (s32[]{:T(128)}, s32[]{:T(128)}, bf16[16384]{0:T(1024)(128)(2,1)S(1)}, bf16[192,512]{1,0:T(8,128)(2,1)S(1)}, f32[192,1024]{1,0:T(8,128)}) %tuple.94), branch_computations={%region_5.5_spmd, %region_6.6_spmd} | conditional | flops 201529344 | bytes 13832302 | solution.py:98
  95.3 2.6 %tile.10 = bf16[785920]{0:T(1024)(128)(2,1)S(1)} reshape(bf16[512,1535]{1,0:T(8,128)(2,1)S(1)} %tile.4) | data formatting | bytes 3143680 | tf_op jit(solution)/shard_map/while/body/eval_jaxpr/cond/branch_1_fun/tile | solution.py:39
  98.0 2.6 %reshape.28 = bf16[512,1534]{1,0:T(8,128)(2,1)S(1)} reshape(bf16[785408]{0:T(1024)(128)(2,1)S(1)} %slice.24) | data formatting | bytes 3141632 | tf_op jit(solution)/shard_map/while/body/eval_jaxpr/cond/branch_1_fun/reshape | solution.py:40
  100.7 2.4 %fusion = f32[192,1024]{1,0:T(8,128)} fusion(f32[192,1024]{1,0:T(8,128)} %get-tuple-element.314, bf16[192,512]{1,0:T(8,128)(2,1)S(1)} %get-tuple-element.318, bf16[512,1534]{1,0:T(8,128)(2,1)S(1)} %reshape.28), kind=kOutput, calls=%fused_computation.1 | convolution fusion | flops 201523200 | bytes 2818048 | tf_op jit(solution)/shard_map/while/body/eval_jaxpr/cond/branch_1_fun/dot_general | solution.py:81
  104.1 8.1 %conditional.4 = (f32[192,1024]{1,0:T(8,128)}) conditional(s32[]{:T(128)} %convert_element_type.31, f32[192,1024]{1,0:T(8,128)} %get-tuple-element.500, (s32[]{:T(128)}, s32[]{:T(128)}, bf16[16384]{0:T(1024)(128)(2,1)S(1)}, bf16[192,512]{1,0:T(8,128)(2,1)S(1)}, f32[192,1024]{1,0:T(8,128)}) %tuple.94), branch_computations={%region_5.5_spmd, %region_6.6_spmd} | conditional | flops 201529344 | bytes 13832302 | solution.py:98
  104.4 2.6 %tile.10 = bf16[785920]{0:T(1024)(128)(2,1)S(1)} reshape(bf16[512,1535]{1,0:T(8,128)(2,1)S(1)} %tile.4) | data formatting | bytes 3143680 | tf_op jit(solution)/shard_map/while/body/eval_jaxpr/cond/branch_1_fun/tile | solution.py:39
  107.1 2.6 %reshape.28 = bf16[512,1534]{1,0:T(8,128)(2,1)S(1)} reshape(bf16[785408]{0:T(1024)(128)(2,1)S(1)} %slice.24) | data formatting | bytes 3141632 | tf_op jit(solution)/shard_map/while/body/eval_jaxpr/cond/branch_1_fun/reshape | solution.py:40
  109.7 2.4 %fusion = f32[192,1024]{1,0:T(8,128)} fusion(f32[192,1024]{1,0:T(8,128)} %get-tuple-element.314, bf16[192,512]{1,0:T(8,128)(2,1)S(1)} %get-tuple-element.318, bf16[512,1534]{1,0:T(8,128)(2,1)S(1)} %reshape.28), kind=kOutput, calls=%fused_computation.1 | convolution fusion | flops 201523200 | bytes 2818048 | tf_op jit(solution)/shard_map/while/body/eval_jaxpr/cond/branch_1_fun/dot_general | solution.py:81
  113.1 8.1 %conditional.4 = (f32[192,1024]{1,0:T(8,128)}) conditional(s32[]{:T(128)} %convert_element_type.31, f32[192,1024]{1,0:T(8,128)} %get-tuple-element.500, (s32[]{:T(128)}, s32[]{:T(128)}, bf16[16384]{0:T(1024)(128)(2,1)S(1)}, bf16[192,512]{1,0:T(8,128)(2,1)S(1)}, f32[192,1024]{1,0:T(8,128)}) %tuple.94), branch_computations={%region_5.5_spmd, %region_6.6_spmd} | conditional | flops 201529344 | bytes 13832302 | solution.py:98
  113.4 2.6 %tile.10 = bf16[785920]{0:T(1024)(128)(2,1)S(1)} reshape(bf16[512,1535]{1,0:T(8,128)(2,1)S(1)} %tile.4) | data formatting | bytes 3143680 | tf_op jit(solution)/shard_map/while/body/eval_jaxpr/cond/branch_1_fun/tile | solution.py:39
  116.1 2.6 %reshape.28 = bf16[512,1534]{1,0:T(8,128)(2,1)S(1)} reshape(bf16[785408]{0:T(1024)(128)(2,1)S(1)} %slice.24) | data formatting | bytes 3141632 | tf_op jit(solution)/shard_map/while/body/eval_jaxpr/cond/branch_1_fun/reshape | solution.py:40
  118.8 2.4 %fusion = f32[192,1024]{1,0:T(8,128)} fusion(f32[192,1024]{1,0:T(8,128)} %get-tuple-element.314, bf16[192,512]{1,0:T(8,128)(2,1)S(1)} %get-tuple-element.318, bf16[512,1534]{1,0:T(8,128)(2,1)S(1)} %reshape.28), kind=kOutput, calls=%fused_computation.1 | convolution fusion | flops 201523200 | bytes 2818048 | tf_op jit(solution)/shard_map/while/body/eval_jaxpr/cond/branch_1_fun/dot_general | solution.py:81
  122.2 8.1 %conditional.4 = (f32[192,1024]{1,0:T(8,128)}) conditional(s32[]{:T(128)} %convert_element_type.31, f32[192,1024]{1,0:T(8,128)} %get-tuple-element.500, (s32[]{:T(128)}, s32[]{:T(128)}, bf16[16384]{0:T(1024)(128)(2,1)S(1)}, bf16[192,512]{1,0:T(8,128)(2,1)S(1)}, f32[192,1024]{1,0:T(8,128)}) %tuple.94), branch_computations={%region_5.5_spmd, %region_6.6_spmd} | conditional | flops 201529344 | bytes 13832302 | solution.py:98
  122.5 2.6 %tile.10 = bf16[785920]{0:T(1024)(128)(2,1)S(1)} reshape(bf16[512,1535]{1,0:T(8,128)(2,1)S(1)} %tile.4) | data formatting | bytes 3143680 | tf_op jit(solution)/shard_map/while/body/eval_jaxpr/cond/branch_1_fun/tile | solution.py:39
  125.2 2.6 %reshape.28 = bf16[512,1534]{1,0:T(8,128)(2,1)S(1)} reshape(bf16[785408]{0:T(1024)(128)(2,1)S(1)} %slice.24) | data formatting | bytes 3141632 | tf_op jit(solution)/shard_map/while/body/eval_jaxpr/cond/branch_1_fun/reshape | solution.py:40
  127.8 2.4 %fusion = f32[192,1024]{1,0:T(8,128)} fusion(f32[192,1024]{1,0:T(8,128)} %get-tuple-element.314, bf16[192,512]{1,0:T(8,128)(2,1)S(1)} %get-tuple-element.318, bf16[512,1534]{1,0:T(8,128)(2,1)S(1)} %reshape.28), kind=kOutput, calls=%fused_computation.1 | convolution fusion | flops 201523200 | bytes 2818048 | tf_op jit(solution)/shard_map/while/body/eval_jaxpr/cond/branch_1_fun/dot_general | solution.py:81
  131.2 8.1 %conditional.4 = (f32[192,1024]{1,0:T(8,128)}) conditional(s32[]{:T(128)} %convert_element_type.31, f32[192,1024]{1,0:T(8,128)} %get-tuple-element.500, (s32[]{:T(128)}, s32[]{:T(128)}, bf16[16384]{0:T(1024)(128)(2,1)S(1)}, bf16[192,512]{1,0:T(8,128)(2,1)S(1)}, f32[192,1024]{1,0:T(8,128)}) %tuple.94), branch_computations={%region_5.5_spmd, %region_6.6_spmd} | conditional | flops 201529344 | bytes 13832302 | solution.py:98
  131.5 2.6 %tile.10 = bf16[785920]{0:T(1024)(128)(2,1)S(1)} reshape(bf16[512,1535]{1,0:T(8,128)(2,1)S(1)} %tile.4) | data formatting | bytes 3143680 | tf_op jit(solution)/shard_map/while/body/eval_jaxpr/cond/branch_1_fun/tile | solution.py:39
  134.3 2.6 %reshape.28 = bf16[512,1534]{1,0:T(8,128)(2,1)S(1)} reshape(bf16[785408]{0:T(1024)(128)(2,1)S(1)} %slice.24) | data formatting | bytes 3141632 | tf_op jit(solution)/shard_map/while/body/eval_jaxpr/cond/branch_1_fun/reshape | solution.py:40
  136.9 2.4 %fusion = f32[192,1024]{1,0:T(8,128)} fusion(f32[192,1024]{1,0:T(8,128)} %get-tuple-element.314, bf16[192,512]{1,0:T(8,128)(2,1)S(1)} %get-tuple-element.318, bf16[512,1534]{1,0:T(8,128)(2,1)S(1)} %reshape.28), kind=kOutput, calls=%fused_computation.1 | convolution fusion | flops 201523200 | bytes 2818048 | tf_op jit(solution)/shard_map/while/body/eval_jaxpr/cond/branch_1_fun/dot_general | solution.py:81
  140.3 8.1 %conditional.4 = (f32[192,1024]{1,0:T(8,128)}) conditional(s32[]{:T(128)} %convert_element_type.31, f32[192,1024]{1,0:T(8,128)} %get-tuple-element.500, (s32[]{:T(128)}, s32[]{:T(128)}, bf16[16384]{0:T(1024)(128)(2,1)S(1)}, bf16[192,512]{1,0:T(8,128)(2,1)S(1)}, f32[192,1024]{1,0:T(8,128)}) %tuple.94), branch_computations={%region_5.5_spmd, %region_6.6_spmd} | conditional | flops 201529344 | bytes 13832302 | solution.py:98
  140.6 2.6 %tile.10 = bf16[785920]{0:T(1024)(128)(2,1)S(1)} reshape(bf16[512,1535]{1,0:T(8,128)(2,1)S(1)} %tile.4) | data formatting | bytes 3143680 | tf_op jit(solution)/shard_map/while/body/eval_jaxpr/cond/branch_1_fun/tile | solution.py:39
  143.3 2.6 %reshape.28 = bf16[512,1534]{1,0:T(8,128)(2,1)S(1)} reshape(bf16[785408]{0:T(1024)(128)(2,1)S(1)} %slice.24) | data formatting | bytes 3141632 | tf_op jit(solution)/shard_map/while/body/eval_jaxpr/cond/branch_1_fun/reshape | solution.py:40
  146.0 2.4 %fusion = f32[192,1024]{1,0:T(8,128)} fusion(f32[192,1024]{1,0:T(8,128)} %get-tuple-element.314, bf16[192,512]{1,0:T(8,128)(2,1)S(1)} %get-tuple-element.318, bf16[512,1534]{1,0:T(8,128)(2,1)S(1)} %reshape.28), kind=kOutput, calls=%fused_computation.1 | convolution fusion | flops 201523200 | bytes 2818048 | tf_op jit(solution)/shard_map/while/body/eval_jaxpr/cond/branch_1_fun/dot_general | solution.py:81
  149.3 8.1 %conditional.4 = (f32[192,1024]{1,0:T(8,128)}) conditional(s32[]{:T(128)} %convert_element_type.31, f32[192,1024]{1,0:T(8,128)} %get-tuple-element.500, (s32[]{:T(128)}, s32[]{:T(128)}, bf16[16384]{0:T(1024)(128)(2,1)S(1)}, bf16[192,512]{1,0:T(8,128)(2,1)S(1)}, f32[192,1024]{1,0:T(8,128)}) %tuple.94), branch_computations={%region_5.5_spmd, %region_6.6_spmd} | conditional | flops 201529344 | bytes 13832302 | solution.py:98
  149.7 2.6 %tile.10 = bf16[785920]{0:T(1024)(128)(2,1)S(1)} reshape(bf16[512,1535]{1,0:T(8,128)(2,1)S(1)} %tile.4) | data formatting | bytes 3143680 | tf_op jit(solution)/shard_map/while/body/eval_jaxpr/cond/branch_1_fun/tile | solution.py:39
  152.4 2.6 %reshape.28 = bf16[512,1534]{1,0:T(8,128)(2,1)S(1)} reshape(bf16[785408]{0:T(1024)(128)(2,1)S(1)} %slice.24) | data formatting | bytes 3141632 | tf_op jit(solution)/shard_map/while/body/eval_jaxpr/cond/branch_1_fun/reshape | solution.py:40
  155.0 2.4 %fusion = f32[192,1024]{1,0:T(8,128)} fusion(f32[192,1024]{1,0:T(8,128)} %get-tuple-element.314, bf16[192,512]{1,0:T(8,128)(2,1)S(1)} %get-tuple-element.318, bf16[512,1534]{1,0:T(8,128)(2,1)S(1)} %reshape.28), kind=kOutput, calls=%fused_computation.1 | convolution fusion | flops 201523200 | bytes 2818048 | tf_op jit(solution)/shard_map/while/body/eval_jaxpr/cond/branch_1_fun/dot_general | solution.py:81
  158.4 8.1 %conditional.4 = (f32[192,1024]{1,0:T(8,128)}) conditional(s32[]{:T(128)} %convert_element_type.31, f32[192,1024]{1,0:T(8,128)} %get-tuple-element.500, (s32[]{:T(128)}, s32[]{:T(128)}, bf16[16384]{0:T(1024)(128)(2,1)S(1)}, bf16[192,512]{1,0:T(8,128)(2,1)S(1)}, f32[192,1024]{1,0:T(8,128)}) %tuple.94), branch_computations={%region_5.5_spmd, %region_6.6_spmd} | conditional | flops 201529344 | bytes 13832302 | solution.py:98
  158.7 2.6 %tile.10 = bf16[785920]{0:T(1024)(128)(2,1)S(1)} reshape(bf16[512,1535]{1,0:T(8,128)(2,1)S(1)} %tile.4) | data formatting | bytes 3143680 | tf_op jit(solution)/shard_map/while/body/eval_jaxpr/cond/branch_1_fun/tile | solution.py:39
  161.4 2.6 %reshape.28 = bf16[512,1534]{1,0:T(8,128)(2,1)S(1)} reshape(bf16[785408]{0:T(1024)(128)(2,1)S(1)} %slice.24) | data formatting | bytes 3141632 | tf_op jit(solution)/shard_map/while/body/eval_jaxpr/cond/branch_1_fun/reshape | solution.py:40
  164.1 2.4 %fusion = f32[192,1024]{1,0:T(8,128)} fusion(f32[192,1024]{1,0:T(8,128)} %get-tuple-element.314, bf16[192,512]{1,0:T(8,128)(2,1)S(1)} %get-tuple-element.318, bf16[512,1534]{1,0:T(8,128)(2,1)S(1)} %reshape.28), kind=kOutput, calls=%fused_computation.1 | convolution fusion | flops 201523200 | bytes 2818048 | tf_op jit(solution)/shard_map/while/body/eval_jaxpr/cond/branch_1_fun/dot_general | solution.py:81
  167.5 8.1 %conditional.4 = (f32[192,1024]{1,0:T(8,128)}) conditional(s32[]{:T(128)} %convert_element_type.31, f32[192,1024]{1,0:T(8,128)} %get-tuple-element.500, (s32[]{:T(128)}, s32[]{:T(128)}, bf16[16384]{0:T(1024)(128)(2,1)S(1)}, bf16[192,512]{1,0:T(8,128)(2,1)S(1)}, f32[192,1024]{1,0:T(8,128)}) %tuple.94), branch_computations={%region_5.5_spmd, %region_6.6_spmd} | conditional | flops 201529344 | bytes 13832302 | solution.py:98
  167.8 2.6 %tile.10 = bf16[785920]{0:T(1024)(128)(2,1)S(1)} reshape(bf16[512,1535]{1,0:T(8,128)(2,1)S(1)} %tile.4) | data formatting | bytes 3143680 | tf_op jit(solution)/shard_map/while/body/eval_jaxpr/cond/branch_1_fun/tile | solution.py:39
  170.5 2.6 %reshape.28 = bf16[512,1534]{1,0:T(8,128)(2,1)S(1)} reshape(bf16[785408]{0:T(1024)(128)(2,1)S(1)} %slice.24) | data formatting | bytes 3141632 | tf_op jit(solution)/shard_map/while/body/eval_jaxpr/cond/branch_1_fun/reshape | solution.py:40
  173.1 2.4 %fusion = f32[192,1024]{1,0:T(8,128)} fusion(f32[192,1024]{1,0:T(8,128)} %get-tuple-element.314, bf16[192,512]{1,0:T(8,128)(2,1)S(1)} %get-tuple-element.318, bf16[512,1534]{1,0:T(8,128)(2,1)S(1)} %reshape.28), kind=kOutput, calls=%fused_computation.1 | convolution fusion | flops 201523200 | bytes 2818048 | tf_op jit(solution)/shard_map/while/body/eval_jaxpr/cond/branch_1_fun/dot_general | solution.py:81
  176.5 8.1 %conditional.4 = (f32[192,1024]{1,0:T(8,128)}) conditional(s32[]{:T(128)} %convert_element_type.31, f32[192,1024]{1,0:T(8,128)} %get-tuple-element.500, (s32[]{:T(128)}, s32[]{:T(128)}, bf16[16384]{0:T(1024)(128)(2,1)S(1)}, bf16[192,512]{1,0:T(8,128)(2,1)S(1)}, f32[192,1024]{1,0:T(8,128)}) %tuple.94), branch_computations={%region_5.5_spmd, %region_6.6_spmd} | conditional | flops 201529344 | bytes 13832302 | solution.py:98
  176.8 2.6 %tile.10 = bf16[785920]{0:T(1024)(128)(2,1)S(1)} reshape(bf16[512,1535]{1,0:T(8,128)(2,1)S(1)} %tile.4) | data formatting | bytes 3143680 | tf_op jit(solution)/shard_map/while/body/eval_jaxpr/cond/branch_1_fun/tile | solution.py:39
  179.5 2.6 %reshape.28 = bf16[512,1534]{1,0:T(8,128)(2,1)S(1)} reshape(bf16[785408]{0:T(1024)(128)(2,1)S(1)} %slice.24) | data formatting | bytes 3141632 | tf_op jit(solution)/shard_map/while/body/eval_jaxpr/cond/branch_1_fun/reshape | solution.py:40
  182.2 2.4 %fusion = f32[192,1024]{1,0:T(8,128)} fusion(f32[192,1024]{1,0:T(8,128)} %get-tuple-element.314, bf16[192,512]{1,0:T(8,128)(2,1)S(1)} %get-tuple-element.318, bf16[512,1534]{1,0:T(8,128)(2,1)S(1)} %reshape.28), kind=kOutput, calls=%fused_computation.1 | convolution fusion | flops 201523200 | bytes 2818048 | tf_op jit(solution)/shard_map/while/body/eval_jaxpr/cond/branch_1_fun/dot_general | solution.py:81
  184.6 1.3 convert_element_type.26
  185.9 2.8 %collective-permute-start = (bf16[192,1024]{1,0:T(8,128)(2,1)S(1)}, bf16[192,1024]{1,0:T(8,128)(2,1)S(1)}, u32[]{:S(2)}, u32[]{:S(2)}) collective-permute-start(bf16[192,1024]{1,0:T(8,128)(2,1)S(1)} %convert_element_type.26), channel_id=1, source_target_pairs={{0,16},{16,0},{4,20},{20,4},{8,24},{24,8},{12,28},{28,12},{1,17},{... | collective-permute-start | bytes 1179656 | tf_op jit(solution)/shard_map/ppermute | solution.py:29
  188.8 2.2 %add_reduce_fusion = s32[8,128]{0,1:T(8,128)S(1)} fusion(s32[192]{0:T(256)S(1)} %get-tuple-element.340, s32[192,8,128]{0,1,2:T(8,128)S(1)} %copy-done.2, s32[192,8]{0,1:T(8,128)S(1)} %slice.29), kind=kLoop, calls=%fused_computation.11 | loop fusion | flops 588800 | bytes 797440 | tf_op jit(solution)/shard_map/reduce_sum | solution.py:53
  191.1 5.2 %all-gather.1 = s32[4,1,1024]{2,1,0:T(1,128)S(1)} all-gather(s32[1,1,1024]{2,1,0:T(1,128)S(1)} %bitcast.32), channel_id=1, replica_groups=mesh['tm'=8,'cell'=4] {'cell'}, dimensions={0}, use_global_device_ids=true | all-gather | bytes 20480 | tf_op jit(solution)/shard_map/all_gather | solution.py:52
  196.9 1.1 broadcast_add_fusion.1
  198.0 1.0 add_multiply_fusion
  (145 shorter events, 21.0 us)
Async XLA Ops:
  7.2 62.6 %all-gather.4.cloned.1.call-start = ((), (), s32[]{:S(2)}) async-start(), calls=%async_computation | async-start | bytes 3538944 | tf_op jit(solution)/shard_map/all_gather | solution.py:71
  57.3 1.0 copy-start.1
  57.5 1.0 copy-start.7
  57.5 11.7 %copy-start.5 = (bf16[8192]{0:T(1024)(128)(2,1)S(1)}, bf16[8192]{0:T(1024)(128)(2,1)}, u32[]{:S(2)}) copy-start(bf16[8192]{0:T(1024)(128)(2,1)} %param.15) | copy-start | bytes 49156
  58.3 13.4 %copy-start.3 = (s32[192,8,128]{2,1,0:T(8,128)}, s32[192,8,128]{2,1,0:T(8,128)S(1)}, u32[]{:S(2)}) copy-start(s32[192,8,128]{2,1,0:T(8,128)S(1)} %copy.13) | copy-start | bytes 2359300
  184.6 4.2 %copy-start.2 = (s32[192,8,128]{0,1,2:T(8,128)S(1)}, s32[192,8,128]{0,1,2:T(8,128)}, u32[]{:S(2)}) copy-start(s32[192,8,128]{0,1,2:T(8,128)} %copy-done.1) | copy-start | bytes 2359300
  184.6 12.3 %copy-start.4 = (s32[192,8,128]{2,1,0:T(8,128)S(1)}, s32[192,8,128]{2,1,0:T(8,128)}, u32[]{:S(2)}) copy-start(s32[192,8,128]{2,1,0:T(8,128)} %copy-done.3) | copy-start | bytes 2359300
  185.9 12.0 %copy-start = (f32[192,1024]{1,0:T(8,128)S(1)}, f32[192,1024]{1,0:T(8,128)}, u32[]{:S(2)}) copy-start(f32[192,1024]{1,0:T(8,128)} %get-tuple-element.341) | copy-start | bytes 2359300
  185.9 12.0 %copy-start.6 = (f32[192]{0:T(256)S(1)}, f32[192]{0:T(256)}, u32[]{:S(2)}) copy-start(f32[192]{0:T(256)} %param.14) | copy-start | bytes 2308
  185.9 12.0 %collective-permute-start = (bf16[192,1024]{1,0:T(8,128)(2,1)S(1)}, bf16[192,1024]{1,0:T(8,128)(2,1)S(1)}, u32[]{:S(2)}, u32[]{:S(2)}) collective-permute-start(bf16[192,1024]{1,0:T(8,128)(2,1)S(1)} %convert_element_type.26), channel_id=1, source_target_pairs={{0,16},{16,0},{4,20},{20,4},{8,24},{24,8},{12,28},{28,12},{1,17},{... | collective-permute-start | bytes 1179656 | tf_op jit(solution)/shard_map/ppermute | solution.py:29
Sparse Core Ops, SparseCore 0:
  10.2 59.4 all-gather.3
where the time goes:
time: 207 us; the launch traced here: 206 us
  local copies, waits for them, and re-layouts  88.4 us (43%)
  other arithmetic  54.1 us (26%)
  matrix products  28.9 us (14%)
  between operations  14.8 us (7%)
  blocking collectives  14.1 us (7%)
  starting transfers between devices  2.87 us (1%)
    another operation x3, other arithmetic  47.7 us
    another operation x24, local copies, waits for them, and re-layouts, toeplitz(): repeated = jnp.tile(pattern, rows_count)[:rows_count * (period - 1)]  32.5 us
    reshape x12, local copies, waits for them, and re-layouts, toeplitz(): return repeated.reshape(rows_count, period - 1)[:, :cols_count]  31.6 us
    dot_general x12, matrix products, product(): return jnp.dot(source_block, matrix, preferred_element_type=jnp.float32)  28.9 us
    dynamic_slice x16, local copies, waits for them, and re-layouts, one_block(): lax.dynamic_slice_in_dim(pieces, index_block * block_len, block_len, 1)  15.1 us
    unnamed x1, blocking collectives  8.95 us
    all_gather x1, blocking collectives, shards(): lax.all_gather(jnp.sum(counts, axis=0, dtype=jnp.int32)[None, :], 'cell',...  5.19 us
  transfers between devices with their start and end apart: 2, of which 1 were waited for; matrix products, arithmetic and copies ran while one was open for 27% of the time, Pallas kernels for 0%

commit v1 on v0

v1 whole, which is shorter than its diff:
```python
import functools

import jax
import jax.numpy as jnp
from jax import lax
from jax.experimental import pallas as pl
from jax.experimental.pallas import tpu as pltpu
from jax.sharding import PartitionSpec as P

MESH = pl.DeviceIdType.MESH
DEPTH = 256
LANES = 128
WIDE = 512


def remote(src, dst, send_sem, recv_sem, target):
    return pltpu.make_async_remote_copy(
        src_ref=src,
        dst_ref=dst,
        send_sem=send_sem,
        recv_sem=recv_sem,
        device_id=target,
        device_id_type=MESH,
    )


def kernel(
    n, m, inc_ref, noise_ref, fac_ref, counts_ref, conv_ref, total_ref,
    held, near, strip, acc, give, got, sums, steps, incb,
    up_send, up_recv, pair_send, pair_recv, sum_send, sum_recv, step_send, step_recv,
):
    rows, seg = noise_ref.shape
    half = rows // 2
    pair = 2 * seg
    me = lax.axis_index("tm")
    cell = lax.axis_index("cell")
    level, side = me // 2, me % 2
    mate = me + 1 - 2 * side
    levels = n // 2

    barrier = pltpu.get_barrier_semaphore()
    for i in range(1, n):
        pl.semaphore_signal(barrier, inc=1, device_id={"tm": lax.rem(me + i, n)}, device_id_type=MESH)
    for i in range(1, m):
        pl.semaphore_signal(barrier, inc=1, device_id={"cell": lax.rem(cell + i, m)}, device_id_type=MESH)
    pl.semaphore_wait(barrier, n + m - 2)

    mine = pl.ds(pl.multiple_of(side * half, 16), half)
    theirs = pl.ds(pl.multiple_of((1 - side) * half, 16), half)

    def lift(q):
        return remote(held.at[q], held.at[q], up_send.at[q], up_recv.at[q], {"tm": jnp.minimum(me + 2, n - 2 + side)})

    def raise_(q):
        @pl.when(level < levels - 1)
        def _():
            lift(q).start()

    swap = remote(noise_ref.at[theirs], held.at[me], pair_send.at[0], pair_recv.at[0], {"tm": mate})
    swap.start()
    rest = remote(noise_ref.at[mine], near, pair_send.at[2], pair_recv.at[2], {"tm": mate})

    @pl.when(side == 0)
    def _():
        rest.start()

    held[me] = noise_ref[mine]
    raise_(me)

    incb[...] = inc_ref[...].astype(jnp.float32).astype(jnp.bfloat16)
    sums[me] = jnp.zeros(sums.shape[1:], jnp.float32)
    sums[me, :, :rows] = lax.dot_general(
        jnp.ones((8, seg), jnp.bfloat16), incb[...], (((1,), (1,)), ((), ())),
        preferred_element_type=jnp.float32,
    )

    def tell(i):
        return remote(sums.at[me], sums.at[me], sum_send.at[i], sum_recv.at[me], {"tm": lax.rem(me + i, n)})

    def heard(i):
        other = lax.rem(me + i, n)
        return remote(sums.at[other], sums.at[other], sum_send.at[i], sum_recv.at[other], {"tm": other})

    for i in range(1, n):
        tell(i).start()

    strip[LANES:, :LANES] = jnp.zeros((LANES, LANES), jnp.bfloat16)

    def lay(chunk):
        at = pl.multiple_of(chunk * seg, LANES)
        slab = fac_ref[:, pl.ds(pl.multiple_of(chunk * seg, LANES), seg + LANES)]
        spread = jnp.broadcast_to(slab, (LANES, seg + LANES))
        skew = pltpu.roll(spread, 0, 1, stride=1, stride_axis=0)[:, LANES:].astype(jnp.bfloat16)
        strip[:LANES, pl.ds(at, seg)] = skew
        strip[LANES:, pl.ds(at + LANES, seg)] = skew

    def convolve(q):
        def part(w, carry):
            cols = pl.ds(pl.multiple_of(w * WIDE, LANES), WIDE)
            total = acc[:, cols]
            for k in range(seg // DEPTH):
                lag = pair * level - seg * q - DEPTH * k
                taps = strip[:, pl.ds(pl.multiple_of(lag + w * WIDE, LANES), WIDE)]
                total += jnp.dot(
                    held[q, :, k * DEPTH : (k + 1) * DEPTH], taps, preferred_element_type=jnp.float32
                )
            acc[:, cols] = total
            return carry

        lax.fori_loop(0, pair // WIDE, part, 0)

    lay(0)
    lay(1)
    acc[...] = jnp.zeros_like(acc)
    conv_ref[...] = jnp.dot(noise_ref[:, :DEPTH], strip[:, :seg], preferred_element_type=jnp.float32)
    for k in range(1, seg // DEPTH):
        conv_ref[:, k * DEPTH :] += jnp.dot(
            noise_ref[:, k * DEPTH : (k + 1) * DEPTH], strip[:, : seg - k * DEPTH], preferred_element_type=jnp.float32
        )
    swap.wait_recv()
    raise_(mate)

    @pl.when(side == 1)
    def _():
        rest.wait_recv()
        for where, block in ((theirs, near), (mine, held.at[mate])):
            total = conv_ref[where]
            for k in range(seg // DEPTH):
                taps = strip[:, seg - k * DEPTH : 2 * seg - k * DEPTH]
                total += jnp.dot(block[:, k * DEPTH : (k + 1) * DEPTH], taps, preferred_element_type=jnp.float32)
            conv_ref[where] = total

    for i in range(1, n):
        heard(i).wait_recv()
    before = jnp.zeros(sums.shape[1:], jnp.float32)
    for q in range(n):
        before += jnp.where(q < me, sums[q], 0.0)
    wide = sums.shape[2]
    diag = lax.broadcasted_iota(jnp.int32, (rows, wide), 0) == lax.broadcasted_iota(jnp.int32, (rows, wide), 1)
    carry = jnp.sum(jnp.where(diag, jnp.broadcast_to(before[0:1], (rows, wide)), 0.0), axis=1, keepdims=True)
    ones = (
        lax.broadcasted_iota(jnp.int32, (DEPTH, DEPTH), 0) <= lax.broadcasted_iota(jnp.int32, (DEPTH, DEPTH), 1)
    ).astype(jnp.float32).astype(jnp.bfloat16)
    for k in range(seg // DEPTH):
        cols = slice(k * DEPTH, (k + 1) * DEPTH)
        run = jnp.dot(incb[:, cols], ones, preferred_element_type=jnp.float32) + carry
        counts_ref[:, cols] = run.astype(jnp.int32)
        steps[cell, :, cols] = jnp.broadcast_to(jnp.sum(run, axis=0, keepdims=True).astype(jnp.int32), (8, DEPTH))
        carry = run[:, DEPTH - 1 :]

    def show(i):
        return remote(steps.at[cell], steps.at[cell], step_send.at[i], step_recv.at[cell], {"cell": lax.rem(cell + i, m)})

    def seen(i):
        other = lax.rem(cell + i, m)
        return remote(steps.at[other], steps.at[other], step_send.at[i], step_recv.at[other], {"cell": other})

    for i in range(1, m):
        show(i).start()

    def step(j, carry):
        lay(2 * j)
        lay(2 * j + 1)
        for q in (2 * (level - j) + side, 2 * (level - j) + 1 - side):
            lift(q).wait_recv()
            raise_(q)
            convolve(q)
        return carry

    lax.fori_loop(1, level + 1, step, 0)

    back = remote(give, got, pair_send.at[1], pair_recv.at[1], {"tm": mate})

    @pl.when(level > 0)
    def _():
        give[...] = acc[:, pl.ds(pl.multiple_of((1 - side) * seg, LANES), seg)].astype(jnp.bfloat16)
        back.start()
        conv_ref[mine] += acc[:, pl.ds(pl.multiple_of(side * seg, LANES), seg)]

    for i in range(1, m):
        seen(i).wait_recv()
    all_steps = steps[0, 0:1]
    for c in range(1, m):
        all_steps += steps[c, 0:1]
    total_ref[...] = all_steps

    @pl.when(level > 0)
    def _():
        back.wait_recv()
        conv_ref[theirs] += got[...].astype(jnp.float32)
        back.wait_send()

    @pl.when(side == 0)
    def _():
        rest.wait_send()

    swap.wait_send()
    for i in range(1, n):
        tell(i).wait_send()
    for i in range(1, m):
        show(i).wait_send()

    @pl.when(level < levels - 1)
    def _():
        def left(q, carry):
            lift(q).wait_send()
            return carry

        lax.fori_loop(0, 2 * level + 2, left, 0)


def solution(mesh):
    n, m = mesh.shape["tm"], mesh.shape["cell"]

    def shards(increments, noise, noise_scale, factor):
        rows, seg = noise.shape
        half = rows // 2
        wide = -(-rows // LANES) * LANES
        fac = jnp.pad(factor.astype(jnp.float32), (LANES, 0))[None, :]
        vmem = pl.BlockSpec(memory_space=pltpu.VMEM)
        dma = pltpu.SemaphoreType.DMA
        counts, conv, total = pl.pallas_call(
            functools.partial(kernel, n, m),
            out_shape=(
                jax.ShapeDtypeStruct((rows, seg), jnp.int32),
                jax.ShapeDtypeStruct((rows, seg), jnp.float32),
                jax.ShapeDtypeStruct((1, seg), jnp.int32),
            ),
            in_specs=[vmem] * 3,
            out_specs=(vmem,) * 3,
            scratch_shapes=[
                pltpu.VMEM((n, half, seg), jnp.bfloat16),
                pltpu.VMEM((half, seg), jnp.bfloat16),
                pltpu.VMEM((DEPTH, n * seg + LANES), jnp.bfloat16),
                pltpu.VMEM((half, 2 * seg), jnp.float32),
                pltpu.VMEM((half, seg), jnp.bfloat16),
                pltpu.VMEM((half, seg), jnp.bfloat16),
                pltpu.VMEM((n, 8, wide), jnp.float32),
                pltpu.VMEM((m, 8, seg), jnp.int32),
                pltpu.VMEM((rows, seg), jnp.bfloat16),
                dma((n,)), dma((n,)), dma((3,)), dma((3,)), dma((n,)), dma((n,)), dma((m,)), dma((m,)),
            ],
            compiler_params=pltpu.CompilerParams(
                collective_id=0, has_side_effects=True, vmem_limit_bytes=50 * 2**20
            ),
        )(increments, noise, fac)
        return counts, noise_scale[:, None] * conv, total[0]

    return jax.shard_map(
        shards,
        mesh=mesh,
        in_specs=(P("cell", "tm"), P("cell", "tm"), P("cell"), P()),
        out_specs=(P("cell", "tm"), P("cell", "tm"), P("tm")),
        check_vma=False,
    )
```

time: 207 us -> 45 us (0.22)
  the two profiles are of different devices: /device:TPU:28 before, /device:TPU:26 now
where the time goes in v1:
time: 45 us; the launch traced here: 44.7 us
  Pallas kernels  38.1 us (85%)
  local copies, waits for them, and re-layouts  4.29 us (10%)
  other arithmetic  1.72 us (4%)
  between operations  0.66 us (1%)
    pallas_call x1, Pallas kernels, shards(): pl.pallas_call(functools.partial(kernel, n, m), out_shape=(jax.ShapeDtype...  38.1 us
    unnamed x8, local copies, waits for them, and re-layouts  4.27 us
    mul x1, other arithmetic, shards(): return (counts, noise_scale[:, None] * conv, total[0])  1 us

profile of v1, /device:TPU:26, one launch (start us, length us, event | category | flops | bytes accessed | tf_op | source)
XLA Modules:
  0.0 44.7 jit_solution(18353260849513010942)
XLA Ops:
  0.6 0.7 %pad_convert_fusion = f32[8320]{0:T(1024)S(1)} fusion(bf16[8192]{0:T(1024)(128)(2,1)} %param.7), kind=kLoop, calls=%fused_computation.1 | loop fusion | flops 8320 | bytes 49664 | tf_op jit(solution)/shard_map/broadcast_in_dim | solution.py:219
  1.4 0.0 copy-start
  1.4 1.1 %copy-done = s32[192,1024]{1,0:T(8,128)S(1)} copy-done((s32[192,1024]{1,0:T(8,128)S(1)}, s32[192,1024]{1,0:T(8,128)}, u32[]{:S(2)}) %copy-start) | copy-done | bytes 786456
  2.5 0.0 copy-start.1
  2.5 1.0 %copy-done.1 = bf16[192,1024]{1,0:T(8,128)(2,1)S(1)} copy-done((bf16[192,1024]{1,0:T(8,128)(2,1)S(1)}, bf16[192,1024]{1,0:T(8,128)(2,1)}, u32[]{:S(2)}) %copy-start.1) | copy-done | bytes 393240
  3.5 38.1 %shard_map.67 = (s32[192,1024]{1,0:T(8,128)S(1)}, f32[192,1024]{1,0:T(8,128)S(1)}, s32[1,1024]{1,0:T(1,128)S(1)}) custom-call(s32[192,1024]{1,0:T(8,128)S(1)} %copy-done, bf16[192,1024]{1,0:T(8,128)(2,1)S(1)} %copy-done.1, f32[1,8320]{1,0:T(1,128)S(1)} %reshape.7.fac_ref), custom_call_target="tpu_custom_call" | custom-call | tf_op jit(solution)/shard_map/pallas_call | solution.py:222
  41.6 0.0 copy-start.2
  41.6 0.7 %copy-done.2 = f32[192]{0:T(256)S(1)} copy-done((f32[192]{0:T(256)S(1)}, f32[192]{0:T(256)}, u32[]{:S(2)}) %copy-start.2) | copy-done | bytes 792
  42.3 1.0 %broadcast_multiply_fusion = f32[192,1024]{1,0:T(8,128)} fusion(f32[192,1024]{1,0:T(8,128)S(1)} %get-tuple-element.7, f32[192]{0:T(256)S(1)} %copy-done.2), kind=kLoop, calls=%fused_computation | loop fusion | flops 196608 | bytes 1573632 | tf_op jit(solution)/shard_map/mul | solution.py:247
  43.3 0.9 %copy.9 = s32[192,1024]{1,0:T(8,128)} copy(s32[192,1024]{1,0:T(8,128)S(1)} %get-tuple-element.12) | data formatting | bytes 1572864
  44.1 0.6 %copy.10 = s32[1024]{0:T(1024)} copy(s32[1024]{0:T(1024)S(1)} %bitcast.1) | data formatting | bytes 8192
  (1 shorter events, 0.0 us)
Async XLA Ops:
  1.4 1.1 %copy-start = (s32[192,1024]{1,0:T(8,128)S(1)}, s32[192,1024]{1,0:T(8,128)}, u32[]{:S(2)}) copy-start(s32[192,1024]{1,0:T(8,128)} %inc_ref.1) | copy-start | bytes 2359300
  2.5 1.0 %copy-start.1 = (bf16[192,1024]{1,0:T(8,128)(2,1)S(1)}, bf16[192,1024]{1,0:T(8,128)(2,1)}, u32[]{:S(2)}) copy-start(bf16[192,1024]{1,0:T(8,128)(2,1)} %noise_ref.1) | copy-start | bytes 1179652
  41.6 0.7 %copy-start.2 = (f32[192]{0:T(256)S(1)}, f32[192]{0:T(256)}, u32[]{:S(2)}) copy-start(f32[192]{0:T(256)} %param.6) | copy-start | bytes 2308

commit v2 on v1

--- a/solution.py
+++ b/solution.py
@@ -25,11 +25,11 @@
 
 
 def kernel(
-    n, m, inc_ref, noise_ref, fac_ref, counts_ref, conv_ref, total_ref,
-    held, near, strip, acc, give, got, sums, steps, incb,
+    n, m, inc_hbm, noise_hbm, scale_ref, fac_ref, counts_ref, conv_ref, total_ref,
+    inc_ref, noise_ref, fetch, held, near, strip, acc, give, got, sums, steps, incb, gains,
     up_send, up_recv, pair_send, pair_recv, sum_send, sum_recv, step_send, step_recv,
 ):
-    rows, seg = noise_ref.shape
+    rows, seg = noise_hbm.shape
     half = rows // 2
     pair = 2 * seg
     me = lax.axis_index("tm")
@@ -38,11 +38,22 @@
     mate = me + 1 - 2 * side
     levels = n // 2
 
+    noise_in = pltpu.make_async_copy(noise_hbm, noise_ref, fetch.at[0])
+    inc_in = pltpu.make_async_copy(inc_hbm, inc_ref, fetch.at[1])
+    noise_in.start()
+    inc_in.start()
     barrier = pltpu.get_barrier_semaphore()
     for i in range(1, n):
         pl.semaphore_signal(barrier, inc=1, device_id={"tm": lax.rem(me + i, n)}, device_id_type=MESH)
     for i in range(1, m):
         pl.semaphore_signal(barrier, inc=1, device_id={"cell": lax.rem(cell + i, m)}, device_id_type=MESH)
+    wide = sums.shape[2]
+    diag = lax.broadcasted_iota(jnp.int32, (rows, wide), 0) == lax.broadcasted_iota(jnp.int32, (rows, wide), 1)
+
+    def column(row):
+        return jnp.sum(jnp.where(diag, jnp.broadcast_to(row, (rows, wide)), 0.0), axis=1, keepdims=True)
+
+    noise_in.wait()
     pl.semaphore_wait(barrier, n + m - 2)
 
     mine = pl.ds(pl.multiple_of(side * half, 16), half)
@@ -59,13 +70,9 @@
     swap = remote(noise_ref.at[theirs], held.at[me], pair_send.at[0], pair_recv.at[0], {"tm": mate})
     swap.start()
     rest = remote(noise_ref.at[mine], near, pair_send.at[2], pair_recv.at[2], {"tm": mate})
-
-    @pl.when(side == 0)
-    def _():
-        rest.start()
-
     held[me] = noise_ref[mine]
     raise_(me)
+    inc_in.wait()
 
     incb[...] = inc_ref[...].astype(jnp.float32).astype(jnp.bfloat16)
     sums[me] = jnp.zeros(sums.shape[1:], jnp.float32)
@@ -83,6 +90,10 @@
 
     for i in range(1, n):
         tell(i).start()
+
+    @pl.when(side == 0)
+    def _():
+        rest.start()
 
     strip[LANES:, :LANES] = jnp.zeros((LANES, LANES), jnp.bfloat16)
 
@@ -135,9 +146,7 @@
     before = jnp.zeros(sums.shape[1:], jnp.float32)
     for q in range(n):
         before += jnp.where(q < me, sums[q], 0.0)
-    wide = sums.shape[2]
-    diag = lax.broadcasted_iota(jnp.int32, (rows, wide), 0) == lax.broadcasted_iota(jnp.int32, (rows, wide), 1)
-    carry = jnp.sum(jnp.where(diag, jnp.broadcast_to(before[0:1], (rows, wide)), 0.0), axis=1, keepdims=True)
+    carry = column(before[0:1])
     ones = (
         lax.broadcasted_iota(jnp.int32, (DEPTH, DEPTH), 0) <= lax.broadcasted_iota(jnp.int32, (DEPTH, DEPTH), 1)
     ).astype(jnp.float32).astype(jnp.bfloat16)
@@ -169,13 +178,19 @@
 
     lax.fori_loop(1, level + 1, step, 0)
 
+    gain = column(scale_ref[...])
+    gains[...] = jnp.broadcast_to(gain, gains.shape)
     back = remote(give, got, pair_send.at[1], pair_recv.at[1], {"tm": mate})
 
     @pl.when(level > 0)
     def _():
         give[...] = acc[:, pl.ds(pl.multiple_of((1 - side) * seg, LANES), seg)].astype(jnp.bfloat16)
         back.start()
-        conv_ref[mine] += acc[:, pl.ds(pl.multiple_of(side * seg, LANES), seg)]
+        conv_ref[mine] = (conv_ref[mine] + acc[:, pl.ds(pl.multiple_of(side * seg, LANES), seg)]) * gains[mine, 0:1]
+
+    @pl.when(level == 0)
+    def _():
+        conv_ref[...] = conv_ref[...] * gains[:, 0:1]
 
     for i in range(1, m):
         seen(i).wait_recv()
@@ -187,7 +202,7 @@
     @pl.when(level > 0)
     def _():
         back.wait_recv()
-        conv_ref[theirs] += got[...].astype(jnp.float32)
+        conv_ref[theirs] = (conv_ref[theirs] + got[...].astype(jnp.float32)) * gains[theirs, 0:1]
         back.wait_send()
 
     @pl.when(side == 0)
@@ -217,6 +232,8 @@
         half = rows // 2
         wide = -(-rows // LANES) * LANES
         fac = jnp.pad(factor.astype(jnp.float32), (LANES, 0))[None, :]
+        hbm = pl.BlockSpec(memory_space=pltpu.HBM)
+        gain = jnp.pad(noise_scale, (0, wide - rows))[None, :]
         vmem = pl.BlockSpec(memory_space=pltpu.VMEM)
         dma = pltpu.SemaphoreType.DMA
         counts, conv, total = pl.pallas_call(
@@ -226,9 +243,12 @@
                 jax.ShapeDtypeStruct((rows, seg), jnp.float32),
                 jax.ShapeDtypeStruct((1, seg), jnp.int32),
             ),
-            in_specs=[vmem] * 3,
+            in_specs=[hbm, hbm, vmem, vmem],
             out_specs=(vmem,) * 3,
             scratch_shapes=[
+                pltpu.VMEM((rows, seg), jnp.int32),
+                pltpu.VMEM((rows, seg), jnp.bfloat16),
+                dma((2,)),
                 pltpu.VMEM((n, half, seg), jnp.bfloat16),
                 pltpu.VMEM((half, seg), jnp.bfloat16),
                 pltpu.VMEM((DEPTH, n * seg + LANES), jnp.bfloat16),
@@ -238,13 +258,14 @@
                 pltpu.VMEM((n, 8, wide), jnp.float32),
                 pltpu.VMEM((m, 8, seg), jnp.int32),
                 pltpu.VMEM((rows, seg), jnp.bfloat16),
+                pltpu.VMEM((rows, LANES), jnp.float32),
                 dma((n,)), dma((n,)), dma((3,)), dma((3,)), dma((n,)), dma((n,)), dma((m,)), dma((m,)),
             ],
             compiler_params=pltpu.CompilerParams(
                 collective_id=0, has_side_effects=True, vmem_limit_bytes=50 * 2**20
             ),
-        )(increments, noise, fac)
-        return counts, noise_scale[:, None] * conv, total[0]
+        )(increments, noise, gain, fac)
+        return counts, conv, total[0]
 
     return jax.shard_map(
         shards,

time: 45 us -> 45.5 us (1.011)
  other arithmetic: 1.72 us -> 0.72 us
  local copies, waits for them, and re-layouts: 4.29 us -> 5.19 us
  Pallas kernels: 38.1 us -> 38.7 us
    mul x1 -> x0, other arithmetic: 1 us -> none  [shards(): return (counts, noise_scale[:, None] * conv, total[0])]
    pad x0 -> x1, local copies, waits for them, and re-layouts: none -> 0.68 us  [shards(): gain = jnp.pad(noise_scale, (0, wide - rows))[None, :]]
    pallas_call x1, Pallas kernels: 38.1 us -> 38.7 us  [shards(): pl.pallas_call(functools.partial(kernel, n, m), out_shape=(jax.ShapeDtype...]
    unnamed x8 -> x7, local copies, waits for them, and re-layouts: 4.27 us -> 4.48 us
where the time goes in v2:
time: 45.5 us; the launch traced here: 45.2 us
  Pallas kernels  38.7 us (85%)
  local copies, waits for them, and re-layouts  5.19 us (11%)
  other arithmetic  0.72 us (2%)
  between operations  0.65 us (1%)
    pallas_call x1, Pallas kernels, shards(): pl.pallas_call(functools.partial(kernel, n, m), out_shape=(jax.ShapeDtype...  38.7 us
    unnamed x7, local copies, waits for them, and re-layouts  4.48 us

profile of v2, /device:TPU:26, one launch (start us, length us, event | category | flops | bytes accessed | tf_op | source)
XLA Modules:
  0.0 45.2 jit_solution(7745391798182883478)
XLA Ops:
  0.6 0.7 %pad.9 = f32[256]{0:T(256)S(1)} pad(f32[192]{0:T(256)} %param.6, f32[]{:T(128)} %constant.3.clone.1), padding=0_64 | pad | bytes 1796 | tf_op jit(solution)/shard_map/jit(_pad)/pad | solution.py:236
  1.3 0.7 %pad_convert_fusion = f32[8320]{0:T(1024)S(1)} fusion(bf16[8192]{0:T(1024)(128)(2,1)} %param.7), kind=kLoop, calls=%fused_computation | loop fusion | flops 8320 | bytes 49664 | tf_op jit(solution)/shard_map/broadcast_in_dim | solution.py:234
  2.1 0.0 copy-start
  2.1 1.1 %copy-done = s32[192,1024]{1,0:T(8,128)S(1)} copy-done((s32[192,1024]{1,0:T(8,128)S(1)}, s32[192,1024]{1,0:T(8,128)}, u32[]{:S(2)}) %copy-start) | copy-done | bytes 786456
  3.2 0.0 copy-start.1
  3.2 1.0 %copy-done.1 = bf16[192,1024]{1,0:T(8,128)(2,1)S(1)} copy-done((bf16[192,1024]{1,0:T(8,128)(2,1)S(1)}, bf16[192,1024]{1,0:T(8,128)(2,1)}, u32[]{:S(2)}) %copy-start.1) | copy-done | bytes 393240
  4.2 38.7 %shard_map.67 = (s32[192,1024]{1,0:T(8,128)S(1)}, f32[192,1024]{1,0:T(8,128)S(1)}, s32[1,1024]{1,0:T(1,128)S(1)}) custom-call(s32[192,1024]{1,0:T(8,128)S(1)} %copy-done, bf16[192,1024]{1,0:T(8,128)(2,1)S(1)} %copy-done.1, f32[1,256]{1,0:T(1,128)S(1)} %bitcast.2, f32[1,8320]{1,0:T(1,128)S(1)} %reshape.6.fac_ref), custom_call_target="tpu_custom_call" | custom-call | tf_op jit(solution)/shard_map/pallas_call | solution.py:239
  42.9 0.9 %copy.10 = s32[192,1024]{1,0:T(8,128)} copy(s32[192,1024]{1,0:T(8,128)S(1)} %get-tuple-element.12) | data formatting | bytes 1572864
  43.7 0.9 %copy.11 = f32[192,1024]{1,0:T(8,128)} copy(f32[192,1024]{1,0:T(8,128)S(1)} %get-tuple-element.13) | data formatting | bytes 1572864
  44.6 0.6 %copy.12 = s32[1024]{0:T(1024)} copy(s32[1024]{0:T(1024)S(1)} %bitcast.3) | data formatting | bytes 8192
  (1 shorter events, 0.0 us)
Async XLA Ops:
  2.1 1.1 %copy-start = (s32[192,1024]{1,0:T(8,128)S(1)}, s32[192,1024]{1,0:T(8,128)}, u32[]{:S(2)}) copy-start(s32[192,1024]{1,0:T(8,128)} %inc_hbm.1) | copy-start | bytes 2359300
  3.2 1.0 %copy-start.1 = (bf16[192,1024]{1,0:T(8,128)(2,1)S(1)}, bf16[192,1024]{1,0:T(8,128)(2,1)}, u32[]{:S(2)}) copy-start(bf16[192,1024]{1,0:T(8,128)(2,1)} %noise_hbm.1) | copy-start | bytes 1179652

commit v3 on v2

--- a/solution.py
+++ b/solution.py
@@ -120,16 +120,23 @@
 
         lax.fori_loop(0, pair // WIDE, part, 0)
 
+    first = 2 * (level - 1) + side
+    acc[...] = jnp.zeros_like(acc)
+    swap.wait_recv()
+    raise_(mate)
+
+    @pl.when(level > 0)
+    def _():
+        lift(first).wait_recv()
+        raise_(first)
+
     lay(0)
     lay(1)
-    acc[...] = jnp.zeros_like(acc)
     conv_ref[...] = jnp.dot(noise_ref[:, :DEPTH], strip[:, :seg], preferred_element_type=jnp.float32)
     for k in range(1, seg // DEPTH):
         conv_ref[:, k * DEPTH :] += jnp.dot(
             noise_ref[:, k * DEPTH : (k + 1) * DEPTH], strip[:, : seg - k * DEPTH], preferred_element_type=jnp.float32
         )
-    swap.wait_recv()
-    raise_(mate)
 
     @pl.when(side == 1)
     def _():
@@ -140,6 +147,35 @@
                 taps = strip[:, seg - k * DEPTH : 2 * seg - k * DEPTH]
                 total += jnp.dot(block[:, k * DEPTH : (k + 1) * DEPTH], taps, preferred_element_type=jnp.float32)
             conv_ref[where] = total
+
+    def step(j, carry):
+        lay(2 * j)
+        lay(2 * j + 1)
+        for q in (2 * (level - j) + side, 2 * (level - j) + 1 - side):
+
+            @pl.when(q != first)
+            def _():
+                lift(q).wait_recv()
+                raise_(q)
+
+            convolve(q)
+        return carry
+
+    lax.fori_loop(1, level + 1, step, 0)
+
+    gain = column(scale_ref[...])
+    gains[...] = jnp.broadcast_to(gain, gains.shape)
+    back = remote(give, got, pair_send.at[1], pair_recv.at[1], {"tm": mate})
+
+    @pl.when(level > 0)
+    def _():
+        give[...] = acc[:, pl.ds(pl.multiple_of((1 - side) * seg, LANES), seg)].astype(jnp.bfloat16)
+        back.start()
+        conv_ref[mine] = (conv_ref[mine] + acc[:, pl.ds(pl.multiple_of(side * seg, LANES), seg)]) * gains[mine, 0:1]
+
+    @pl.when(level == 0)
+    def _():
+        conv_ref[...] = conv_ref[...] * gains[:, 0:1]
 
     for i in range(1, n):
         heard(i).wait_recv()
@@ -166,31 +202,6 @@
 
     for i in range(1, m):
         show(i).start()
-
-    def step(j, carry):
-        lay(2 * j)
-        lay(2 * j + 1)
-        for q in (2 * (level - j) + side, 2 * (level - j) + 1 - side):
-            lift(q).wait_recv()
-            raise_(q)
-            convolve(q)
-        return carry
-
-    lax.fori_loop(1, level + 1, step, 0)
-
-    gain = column(scale_ref[...])
-    gains[...] = jnp.broadcast_to(gain, gains.shape)
-    back = remote(give, got, pair_send.at[1], pair_recv.at[1], {"tm": mate})
-
-    @pl.when(level > 0)
-    def _():
-        give[...] = acc[:, pl.ds(pl.multiple_of((1 - side) * seg, LANES), seg)].astype(jnp.bfloat16)
-        back.start()
-        conv_ref[mine] = (conv_ref[mine] + acc[:, pl.ds(pl.multiple_of(side * seg, LANES), seg)]) * gains[mine, 0:1]
-
-    @pl.when(level == 0)
-    def _():
-        conv_ref[...] = conv_ref[...] * gains[:, 0:1]
 
     for i in range(1, m):
         seen(i).wait_recv()
@@ -262,7 +273,7 @@
                 dma((n,)), dma((n,)), dma((3,)), dma((3,)), dma((n,)), dma((n,)), dma((m,)), dma((m,)),
             ],
             compiler_params=pltpu.CompilerParams(
-                collective_id=0, has_side_effects=True, vmem_limit_bytes=50 * 2**20
+                collective_id=0, has_side_effects=True, vmem_limit_bytes=52 * 2**20
             ),
         )(increments, noise, gain, fac)
         return counts, conv, total[0]

time: 45.5 us -> 43.3 us (0.952)
  the two profiles are of different devices: /device:TPU:26 before, /device:TPU:28 now
where the time goes in v3:
time: 43.3 us; the launch traced here: 43.1 us
  Pallas kernels  37.7 us (87%)
  local copies, waits for them, and re-layouts  4.05 us (9%)
  other arithmetic  0.72 us (2%)
  between operations  0.65 us (2%)
    pallas_call x1, Pallas kernels, shards(): pl.pallas_call(functools.partial(kernel, n, m), out_shape=(jax.ShapeDtype...  37.7 us
    unnamed x5, local copies, waits for them, and re-layouts  3.35 us

profile of v3, /device:TPU:28, one launch (start us, length us, event | category | flops | bytes accessed | tf_op | source)
XLA Modules:
  0.0 43.1 jit_solution(9732287712855608669)
XLA Ops:
  0.6 0.7 %pad.9 = f32[256]{0:T(256)S(1)} pad(f32[192]{0:T(256)} %param.6, f32[]{:T(128)} %constant.3.clone.1), padding=0_64 | pad | bytes 1796 | tf_op jit(solution)/shard_map/jit(_pad)/pad | solution.py:247
  1.3 0.7 %pad_convert_fusion = f32[8320]{0:T(1024)S(1)} fusion(bf16[8192]{0:T(1024)(128)(2,1)} %param.7), kind=kLoop, calls=%fused_computation | loop fusion | flops 8320 | bytes 49664 | tf_op jit(solution)/shard_map/broadcast_in_dim | solution.py:245
  2.1 0.0 copy-start
  2.1 1.0 %copy-done = bf16[192,1024]{1,0:T(8,128)(2,1)S(1)} copy-done((bf16[192,1024]{1,0:T(8,128)(2,1)S(1)}, bf16[192,1024]{1,0:T(8,128)(2,1)}, u32[]{:S(2)}) %copy-start) | copy-done | bytes 393240
  3.1 37.7 %shard_map.67 = (s32[192,1024]{1,0:T(8,128)S(1)}, f32[192,1024]{1,0:T(8,128)S(1)}, s32[1,1024]{1,0:T(1,128)S(1)}) custom-call(s32[192,1024]{1,0:T(8,128)} %inc_hbm.1, bf16[192,1024]{1,0:T(8,128)(2,1)S(1)} %copy-done, f32[1,256]{1,0:T(1,128)S(1)} %bitcast.2, f32[1,8320]{1,0:T(1,128)S(1)} %reshape.6.fac_ref), custom_call_target="tpu_custom_call" | custom-call | tf_op jit(solution)/shard_map/pallas_call | solution.py:250
  40.7 0.9 %copy.10 = s32[192,1024]{1,0:T(8,128)} copy(s32[192,1024]{1,0:T(8,128)S(1)} %get-tuple-element.12) | data formatting | bytes 1572864
  41.6 0.9 %copy.11 = f32[192,1024]{1,0:T(8,128)} copy(f32[192,1024]{1,0:T(8,128)S(1)} %get-tuple-element.13) | data formatting | bytes 1572864
  42.5 0.6 %copy.12 = s32[1024]{0:T(1024)} copy(s32[1024]{0:T(1024)S(1)} %bitcast.3) | data formatting | bytes 8192
  (1 shorter events, 0.0 us)
Async XLA Ops:
  2.1 1.0 %copy-start = (bf16[192,1024]{1,0:T(8,128)(2,1)S(1)}, bf16[192,1024]{1,0:T(8,128)(2,1)}, u32[]{:S(2)}) copy-start(bf16[192,1024]{1,0:T(8,128)(2,1)} %noise_hbm.1) | copy-start | bytes 1179652

commit v4 on v3

--- a/solution.py
+++ b/solution.py
@@ -47,11 +47,10 @@
         pl.semaphore_signal(barrier, inc=1, device_id={"tm": lax.rem(me + i, n)}, device_id_type=MESH)
     for i in range(1, m):
         pl.semaphore_signal(barrier, inc=1, device_id={"cell": lax.rem(cell + i, m)}, device_id_type=MESH)
-    wide = sums.shape[2]
-    diag = lax.broadcasted_iota(jnp.int32, (rows, wide), 0) == lax.broadcasted_iota(jnp.int32, (rows, wide), 1)
+    diag = lax.broadcasted_iota(jnp.int32, (rows, rows), 0) == lax.broadcasted_iota(jnp.int32, (rows, rows), 1)
 
     def column(row):
-        return jnp.sum(jnp.where(diag, jnp.broadcast_to(row, (rows, wide)), 0.0), axis=1, keepdims=True)
+        return jnp.sum(jnp.where(diag, jnp.broadcast_to(row, (rows, rows)), 0.0), axis=1, keepdims=True)
 
     noise_in.wait()
     pl.semaphore_wait(barrier, n + m - 2)
@@ -182,7 +181,7 @@
     before = jnp.zeros(sums.shape[1:], jnp.float32)
     for q in range(n):
         before += jnp.where(q < me, sums[q], 0.0)
-    carry = column(before[0:1])
+    carry = column(before[0:1, :rows])
     ones = (
         lax.broadcasted_iota(jnp.int32, (DEPTH, DEPTH), 0) <= lax.broadcasted_iota(jnp.int32, (DEPTH, DEPTH), 1)
     ).astype(jnp.float32).astype(jnp.bfloat16)
@@ -244,7 +243,7 @@
         wide = -(-rows // LANES) * LANES
         fac = jnp.pad(factor.astype(jnp.float32), (LANES, 0))[None, :]
         hbm = pl.BlockSpec(memory_space=pltpu.HBM)
-        gain = jnp.pad(noise_scale, (0, wide - rows))[None, :]
+        gain = noise_scale[None, :]
         vmem = pl.BlockSpec(memory_space=pltpu.VMEM)
         dma = pltpu.SemaphoreType.DMA
         counts, conv, total = pl.pallas_call(

time: 43.3 us -> 43.3 us (level)
    pad x1 -> x0, local copies, waits for them, and re-layouts: 0.68 us -> none  [shards(): gain = jnp.pad(noise_scale, (0, wide - rows))[None, :]]
    unnamed x5 -> x7, local copies, waits for them, and re-layouts: 3.35 us -> 4 us
where the time goes in v4:
time: 43.3 us; the launch traced here: 43.1 us
  Pallas kernels  37.7 us (87%)
  local copies, waits for them, and re-layouts  4.02 us (9%)
  other arithmetic  0.72 us (2%)
  between operations  0.64 us (1%)
    pallas_call x1, Pallas kernels, shards(): pl.pallas_call(functools.partial(kernel, n, m), out_shape=(jax.ShapeDtype...  37.7 us
    unnamed x7, local copies, waits for them, and re-layouts  4 us

profile of v4, /device:TPU:28, one launch (start us, length us, event | category | flops | bytes accessed | tf_op | source)
XLA Modules:
  0.0 43.1 jit_solution(15630169927850763438)
XLA Ops:
  0.6 0.7 %pad_convert_fusion = f32[8320]{0:T(1024)S(1)} fusion(bf16[8192]{0:T(1024)(128)(2,1)} %param.7), kind=kLoop, calls=%fused_computation | loop fusion | flops 8320 | bytes 49664 | tf_op jit(solution)/shard_map/broadcast_in_dim | solution.py:244
  1.4 0.0 copy-start.1
  1.4 0.7 %copy-done.1 = f32[192]{0:T(256)S(1)} copy-done((f32[192]{0:T(256)S(1)}, f32[192]{0:T(256)}, u32[]{:S(2)}) %copy-start.1) | copy-done | bytes 792
  2.0 0.0 copy-start
  2.0 1.0 %copy-done = bf16[192,1024]{1,0:T(8,128)(2,1)S(1)} copy-done((bf16[192,1024]{1,0:T(8,128)(2,1)S(1)}, bf16[192,1024]{1,0:T(8,128)(2,1)}, u32[]{:S(2)}) %copy-start) | copy-done | bytes 393240
  3.0 37.7 %shard_map.67 = (s32[192,1024]{1,0:T(8,128)S(1)}, f32[192,1024]{1,0:T(8,128)S(1)}, s32[1,1024]{1,0:T(1,128)S(1)}) custom-call(s32[192,1024]{1,0:T(8,128)} %inc_hbm.1, bf16[192,1024]{1,0:T(8,128)(2,1)S(1)} %copy-done, f32[1,192]{1,0:T(1,128)S(1)} %bitcast.3, f32[1,8320]{1,0:T(1,128)S(1)} %reshape.6.fac_ref), custom_call_target="tpu_custom_call" | custom-call | tf_op jit(solution)/shard_map/pallas_call | solution.py:249
  40.7 0.9 %copy.10 = s32[192,1024]{1,0:T(8,128)} copy(s32[192,1024]{1,0:T(8,128)S(1)} %get-tuple-element.12) | data formatting | bytes 1572864
  41.6 0.9 %copy.11 = f32[192,1024]{1,0:T(8,128)} copy(f32[192,1024]{1,0:T(8,128)S(1)} %get-tuple-element.13) | data formatting | bytes 1572864
  42.5 0.6 %copy.12 = s32[1024]{0:T(1024)} copy(s32[1024]{0:T(1024)S(1)} %bitcast.2) | data formatting | bytes 8192
  (1 shorter events, 0.0 us)
Async XLA Ops:
  1.4 0.7 %copy-start.1 = (f32[192]{0:T(256)S(1)}, f32[192]{0:T(256)}, u32[]{:S(2)}) copy-start(f32[192]{0:T(256)} %param.6) | copy-start | bytes 2308
  2.0 1.0 %copy-start = (bf16[192,1024]{1,0:T(8,128)(2,1)S(1)}, bf16[192,1024]{1,0:T(8,128)(2,1)}, u32[]{:S(2)}) copy-start(bf16[192,1024]{1,0:T(8,128)(2,1)} %noise_hbm.1) | copy-start | bytes 1179652
